TPU v7x, 512 devices: a whole 4x4x16 slice. The times are simulated.
512 devices in a mesh: dp: 8 (over z_lo), ctx: 64 (over z_hi, y, x, core).
Axes of the slice: x: 4, y: 4, z: 16 (z_hi: 2, z_lo: 8; z = z_hi * 8 + z_lo), core: 2. Of those that a mesh axis runs over, the one named last changes fastest.
Arguments:
- fwd_proj: bfloat16 [65536, 3072], P(('dp', 'ctx')), parts along dimension 0, may hold values from -6 to 6
- rev_proj: bfloat16 [65536, 3072], P(('dp', 'ctx')), parts along dimension 0, may hold values from -6 to 6
- tokens: int32 [65536], P(('dp', 'ctx')), parts along dimension 0, may hold values from 0 to 4
- short_taps: float32 [3, 3072], replicated, may hold values from -3.5 to 3.5
- long_kernel: float32 [1024, 8192], P('ctx'), may hold values from -1 to 1
- skip_gain: float32 [1024], P('ctx'), may hold values from -4 to 4
- out_weight: bfloat16 [1024, 1024], replicated, may hold values from -0.1875 to 0.1875
Outputs:
- mixed: bfloat16 [65536, 1024], P(('dp', 'ctx')), parts along dimension 0
There are 8 independent parts, one for each index of `dp`. A program takes and returns all parts, laid end to end along the dimension named above; an argument that names none is the same for every part. Nothing has to cross between parts.
Inputs may be any that keep to these rules, and one draw needn't show every extreme that they name: `tokens`: base of each position, 0 to 3 for A, C, G, T and 4 for an unknown base N.
All inputs are finite; a program needn't handle non-finite values.
Results may differ from a plain program's by a relative error of at most 0.0064.
Values may be sent and summed in bfloat16 or wider, within the bound.
A program may use at most 64 MiB of HBM per device.

v0:
```python
import jax
import jax.numpy as jnp
from jax import lax
from jax.experimental import pallas as pl
from jax.experimental.pallas import tpu as pltpu
from jax.sharding import PartitionSpec as P

F32, BF16, I32 = jnp.float32, jnp.bfloat16, jnp.int32
MESH = pl.DeviceIdType.MESH
D = 1024
POS = 128
NB = 32
CH = 16
PAD = 16
ROWS = PAD + NB + PAD
LINE = 8
U = 4


def eye(flip):
    row = lax.broadcasted_iota(I32, (POS, POS), 0)
    col = lax.broadcasted_iota(I32, (POS, POS), 1)
    return (row == jnp.where(flip, POS - 1 - col, col)).astype(F32).astype(BF16)


def lane_below(rows, bound):
    return lax.broadcasted_iota(I32, (rows, 128), 1) < bound


def build_taps(rows_ref, first, count, out):
    row = lax.broadcasted_iota(I32, (8, 128), 0)
    lane = lax.broadcasted_iota(I32, (8, 128), 1)
    masks = [lane >= row + 8 * k for k in range(4)]
    before = [jnp.zeros((8, 128), F32)] * 4
    for j in range(count):
        if j % 16 == 0:
            rows = rows_ref[pl.ds(pl.multiple_of(first + j, 16), 16), :].astype(F32)
        wide = jnp.broadcast_to(rows[j % 16 : j % 16 + 1], (8, 128))
        now = [pltpu.roll(wide, 8 * k, 1, stride=1, stride_axis=0) for k in range(4)]
        at, col = 32 * (j // 2), 128 * (j % 2)
        for k in range(2):
            both = [jnp.where(masks[i], now[i], before[i]) for i in (2 * k, 2 * k + 1)]
            out[at + 16 * k : at + 16 * k + 16, col : col + 128] = jnp.concatenate(
                both, axis=0
            ).astype(BF16)
        before = now


def spread(staged, c, turned):
    x = staged[pl.ds(c, NB, stride=CH), :]
    turned[0, PAD : PAD + NB, :] = x
    for m in range(1, 4):
        turned[m, PAD : PAD + NB, :] = pltpu.roll(x, 32 * m, 1)


def pieces(turned, start, rows):
    for w in range(2):
        for rho in range(4):

            def load(i):
                return turned[(i - rho) % 4, pl.ds(PAD + start - 8 * w - 2 * i, rows), :]

            v = load(3)
            for i in (2, 1, 0):
                v = jnp.where(lane_below(rows, 32 * (i + 1)), load(i), v)
            yield w, rho, v.astype(BF16)


def overlap(part, at):
    def load(rho, off, col):
        return part[rho, pl.ds(at + off, NB), pl.ds(col, 128)]

    y = load(0, 0, 0) + load(0, -1, 128)
    for rho in range(1, 4):
        low = lane_below(NB, 32 * (4 - rho))
        mix = jnp.where(low, load(rho, 0, 0), load(rho, -1, 0)) + jnp.where(
            low, load(rho, -1, 128), load(rho, -2, 128)
        )
        y = y + pltpu.roll(mix, 32 * rho, 1)
    return y


def near_rows(c, sig_a, sig_b, lhs, turned):
    for which, staged in enumerate((sig_a, sig_b)):
        spread(staged, c, turned.at[which])
        for w, rho, v in pieces(turned.at[which], 0, NB):
            base = 4 * NB * which + NB * rho
            for s in range(2):
                lhs[base + 16 * s : base + NB, pl.ds(256 * s + 128 * w, 128)] = v[: NB - 16 * s]


def near_dot(taps, lhs, parts):
    acc = jnp.dot(lhs[...], taps[:512, :], preferred_element_type=F32)
    for i in range(2):
        for rho in range(4):
            at = (4 * i + rho) * NB
            parts[i, rho, 8 : 8 + NB, :] = acc[at : at + NB]


def near_sum(c, parts, out_a, out_b):
    at = pl.ds(c, NB, stride=CH)
    for i, out in enumerate((out_a, out_b)):
        out[at, :] = overlap(parts.at[i], 8)


def far_rows(c, sig, lhs, turned):
    spread(sig, c, turned)
    for w, rho, v in pieces(turned, -2, 48):
        for s in range(4):
            src = 32 - 16 * s
            dst = max(0, -src)
            src = max(0, src)
            count = min(48 - src, 48 - dst)
            at = 48 * rho + dst
            lhs[at : at + count, pl.ds(256 * s + 128 * w, 128)] = v[src : src + count]


def far_dot(taps, lhs, part):
    acc = jnp.dot(lhs[...], taps[...], preferred_element_type=F32)
    for rho in range(4):
        part[rho, :, :] = acc[48 * rho : 48 * rho + 48]


def far_sum(c, part, out, add):
    at = pl.ds(c, NB, stride=CH)
    y = overlap(part, 2)
    out[at, :] = out[at, :] + y if add else y


def kernel(
    fwd, rev, tok, taps, lk, skip, weight, out,
    xin, xf, hsend, halo, z, hf, hk, hn, ho, g, go, rab, rr, sa, sb, sr, ya, yb, ys, ps, yt, pt,
    o, comb, wv, lkv,
    ln0, ln1, ln2, ln3, lf0, lf1, lf2, lf3, tn0, tn1, tn2, tn3, pn0, pn1, pn2, pn3,
    pf0, pf1, pf2, pf3,
    in_sem, halo_s, halo_r, ex_s, ex_r, z_s, z_r, y_s, y_r,
):
    lns, lfs = (ln0, ln1, ln2, ln3), (lf0, lf1, lf2, lf3)
    tns, pns, pfs = (tn0, tn1, tn2, tn3), (pn0, pn1, pn2, pn3), (pf0, pf1, pf2, pf3)
    dp = lax.axis_index("dp")
    ctx = lax.axis_index("ctx")
    h = ctx // NB
    r = ctx - h * NB
    slot = jnp.where(h == 0, r, NB - 1 - r)
    quad = dp // 4
    seat = dp - 4 * quad
    across = (lax.rem(dp + 4, LINE), (1 - h) * NB + r)

    def mate(j):
        return (4 * quad + lax.rem(seat + j, 4), ctx)

    @pl.when(h == 0)
    def _():
        pltpu.make_async_copy(fwd, xin.at[0], in_sem.at[0]).start()
        pltpu.make_async_copy(rev, xin.at[1], in_sem.at[1]).start()

    @pl.when(h == 1)
    def _():
        pltpu.make_async_copy(rev, xin.at[0], in_sem.at[0]).start()
        pltpu.make_async_copy(fwd, xin.at[1], in_sem.at[1]).start()

    pltpu.make_async_copy(lk, lkv, in_sem.at[2]).start()
    pltpu.make_async_copy(weight, wv, in_sem.at[3]).start()

    barrier = pltpu.get_barrier_semaphore()

    def greet(who):
        pl.semaphore_signal(barrier, inc=1, device_id=who, device_id_type=MESH)

    greet(across)

    def greet_far(j, _):
        greet((dp, (1 - h) * NB + lax.rem(r + j, NB)))
        return 0

    def greet_near(j, _):
        greet((dp, h * NB + lax.rem(r + j, NB)))
        return 0

    lax.fori_loop(0, NB, greet_far, 0)
    for j in range(1, 4):
        greet(mate(j))
    lax.fori_loop(1, NB, greet_near, 0)

    for ref in lns + lfs + tns + pns:
        ref[...] = jnp.zeros_like(ref)

    flips = (eye(h == 1), eye(h == 0))
    for role in range(2):
        pltpu.make_async_copy(fwd, xin.at[role], in_sem.at[role]).wait()
        for i in range(6):
            col = pl.ds(512 * i, 512)
            x = jnp.dot(flips[role], xin[role, :, col], preferred_element_type=F32)
            xf[role, 8 : 8 + POS, col] = x
            hsend[role, :, col] = x[POS - 16 :].astype(BF16)

    pltpu.make_async_copy(lk, lkv, in_sem.at[2]).wait()
    diag = lax.broadcasted_iota(I32, (CH, CH), 0) == lax.broadcasted_iota(I32, (CH, CH), 1)
    gain = jnp.sum(jnp.where(diag, skip[...], 0.0), axis=1, keepdims=True)
    first = lax.broadcasted_iota(I32, (CH, 128), 1) == 0
    for j in range(64):
        v = lkv[:, 128 * j : 128 * j + 128]
        if j == 0:
            v = v + jnp.where(first, gain, 0.0)
        hf[pl.ds(j, CH, stride=64), :] = v
    for c in range(CH):
        v = hf[64 * c : 64 * c + 64, :].astype(BF16)
        hk[64 * c : 64 * c + 64, :] = v
        hn[32 * c : 32 * c + 32, :] = v[:32]

    pl.semaphore_wait(barrier, 2 * NB - 1 + 4)

    at_end = slot == NB - 1
    inner = jnp.where(h == 0, r + 1, r - 1)
    turn = jnp.where(h == 0, 0, NB - 1)
    next_a = jnp.where(at_end, (1 - h) * NB + turn, h * NB + inner)
    next_b = h * NB + jnp.where(h == 0, r - 1, r + 1)

    def halo_copy(src, dst, to):
        return pltpu.make_async_remote_copy(
            src_ref=hsend.at[src], dst_ref=halo.at[dst], send_sem=halo_s.at[src],
            recv_sem=halo_r.at[dst], device_id=(dp, to), device_id_type=MESH,
        )

    @pl.when(at_end)
    def _():
        halo_copy(0, 1, next_a).start()

    @pl.when(jnp.logical_not(at_end))
    def _():
        halo_copy(0, 0, next_a).start()

    @pl.when(slot > 0)
    def _():
        halo_copy(1, 1, next_b).start()

    share = pl.ds(pl.multiple_of(seat * 128, 128), 128)
    cross = pltpu.make_async_remote_copy(
        src_ref=hn.at[share], dst_ref=ho.at[share], send_sem=ex_s.at[0], recv_sem=ex_r.at[0],
        device_id=across, device_id_type=MESH,
    )
    cross.start()

    def own(i, _):
        for u in range(U):
            c = i * U + u
            build_taps(hk, c * 64, 64, g.at[c])
        return 0

    lax.fori_loop(0, CH // U, own, 0)

    known = (tok[...] != 4).astype(F32).astype(BF16)
    known = jnp.broadcast_to(known, (16, POS))

    def short(role, col):
        return (
            taps[0:1, col] * xf[role, 8 : 8 + POS, col]
            + taps[1:2, col] * xf[role, 7 : 7 + POS, col]
            + taps[2:3, col] * xf[role, 6 : 6 + POS, col]
        )

    def gate(role):
        mask = jnp.dot(known, flips[role], preferred_element_type=F32)[0:1]

        def tile(i, _):
            v = short(role, pl.ds(pl.multiple_of(128 * i, 128), 128))
            q = short(role, pl.ds(pl.multiple_of(128 * i + D, 128), 128))
            turned = (jnp.transpose(q * v) * mask).astype(BF16)
            z[pl.ds(8 * i, 8), role, :, :] = turned.reshape(8, CH, POS)
            return 0

        lax.fori_loop(0, D // 128, tile, 0)

    @pl.when(slot > 0)
    def _():
        pltpu.make_async_copy(halo.at[0], halo.at[0], halo_r.at[0]).wait()
        xf[0, 0:8, :] = halo[0, :, :].astype(F32)[8:16]

    @pl.when(slot == 0)
    def _():
        xf[0, 0:8, :] = jnp.zeros((8, 3 * D), F32)

    gate(0)

    def send_far(j, _):
        who = lax.rem(r + j, NB)
        pltpu.make_async_remote_copy(
            src_ref=z.at[(1 - h) * NB + who, 0], dst_ref=rr.at[slot],
            send_sem=z_s.at[2], recv_sem=z_r.at[2],
            device_id=(dp, (1 - h) * NB + who), device_id_type=MESH,
        ).start()
        return 0

    lax.fori_loop(0, NB, send_far, 0)

    pltpu.make_async_copy(halo.at[1], halo.at[1], halo_r.at[1]).wait()
    xf[1, 0:8, :] = halo[1, :, :].astype(F32)[8:16]
    gate(1)

    for k in range(2):
        group = h if k == 0 else 1 - h
        pltpu.make_async_copy(z.at[group * NB + r], rab.at[k, slot], z_r.at[k]).start()

        def send_near(j, _, k=k, group=group):
            who = lax.rem(r + j, NB)
            pltpu.make_async_remote_copy(
                src_ref=z.at[group * NB + who], dst_ref=rab.at[k, slot],
                send_sem=z_s.at[k], recv_sem=z_r.at[k],
                device_id=(dp, h * NB + who), device_id_type=MESH,
            ).start()
            return 0

        lax.fori_loop(1, NB, send_near, 0)

    cross.wait_recv()

    def mate_copy(j):
        return pltpu.make_async_remote_copy(
            src_ref=ho.at[share], dst_ref=ho.at[share], send_sem=ex_s.at[j],
            recv_sem=ex_r.at[j], device_id=mate(j), device_id_type=MESH,
        )

    for j in range(1, 4):
        mate_copy(j).start()

    for role in range(2):
        turned = h == 1 - role

        def gate_out(i, _, role=role, turned=turned):
            src = jnp.where(turned, D // 128 - 1 - i, i) * 128
            a = short(role, pl.ds(pl.multiple_of(src + 2 * D, 128), 128))
            high = a.astype(BF16)
            low = (a - high.astype(F32)).astype(BF16)
            both = jnp.concatenate([high, low], axis=1)
            both = jnp.dot(flips[role], both, preferred_element_type=F32).astype(BF16)
            both = jnp.concatenate([both[:, :128], both[:, 128:]], axis=0)
            both = jnp.dot(both, flips[role], preferred_element_type=F32)
            o[role, :, pl.ds(pl.multiple_of(128 * i, 128), 128)] = both[:POS] + both[POS:]
            return 0

        lax.fori_loop(0, D // 128, gate_out, 0)

    def stage(k):
        pltpu.make_async_copy(rab.at[k], rab.at[k], z_r.at[k]).wait()
        for b in range(NB):
            rows = pl.ds(CH * b, CH)
            sa[rows, :] = rab[k, b, 0, :, :].astype(F32)
            sb[rows, :] = rab[k, NB - 1 - b, 1, :, :].astype(F32)

    def near(taps_ref):
        def go(i, _):
            c = i * U
            for u in range(U):
                near_rows(c + u, sa, sb, lns[u], tns[u])
            for u in range(U):
                near_dot(taps_ref.at[c + u], lns[u], pns[u])
            for u in range(U):
                near_sum(c + u, pns[u], ya, yb)
            return 0

        lax.fori_loop(0, CH // U, go, 0)

    def far(sig, dst, add):
        def go(i, _):
            c = i * U
            for u in range(U):
                far_rows(c + u, sig, lfs[u], tns[u].at[0])
            for u in range(U):
                far_dot(g.at[c + u], lfs[u], pfs[u])
            for u in range(U):
                far_sum(c + u, pfs[u], dst, add)
            return 0

        lax.fori_loop(0, CH // U, go, 0)

    def pack_a(k):
        for b in range(NB):
            ys[k, b, 0, :, :] = ya[CH * b : CH * b + CH, :].astype(BF16)

    def pack_b(k):
        for b in range(NB):
            ys[k, NB - 1 - b, 1, :, :] = yb[CH * b : CH * b + CH, :].astype(BF16)

    def give(src, dst, sem):
        pltpu.make_async_copy(src(slot), dst, y_r.at[sem]).start()

        def go(j, _):
            who = lax.rem(r + j, NB)
            at = jnp.where(h == 0, who, NB - 1 - who)
            pltpu.make_async_remote_copy(
                src_ref=src(at), dst_ref=dst, send_sem=y_s.at[sem], recv_sem=y_r.at[sem],
                device_id=(dp, h * NB + who), device_id_type=MESH,
            ).start()
            return 0

        lax.fori_loop(1, NB, go, 0)

    stage(0)
    far(sa, yb, False)
    for b in range(NB):
        ps[b, :, :] = yb[CH * b : CH * b + CH, :].astype(BF16)

    def send_part(j, _):
        who = lax.rem(r + j, NB)
        at = jnp.where(h == 0, who, NB - 1 - who)
        pltpu.make_async_remote_copy(
            src_ref=ps.at[at], dst_ref=pt.at[r], send_sem=y_s.at[3], recv_sem=y_r.at[3],
            device_id=(dp, (1 - h) * NB + who), device_id_type=MESH,
        ).start()
        return 0

    lax.fori_loop(0, NB, send_part, 0)

    near(g)
    pack_a(0)
    give(lambda s: ys.at[0, s, 0], yt.at[h * NB + r, 0], 0)
    pltpu.make_async_copy(rr, rr, z_r.at[2]).wait()
    for b in range(NB):
        sr[CH * b : CH * b + CH, :] = rr[b, :, :].astype(F32)
    far(sr, yb, True)
    pack_b(0)
    give(lambda s: ys.at[0, s, 1], yt.at[h * NB + r, 1], 1)

    for j in range(1, 4):
        rows = pl.ds(pl.multiple_of(lax.rem(seat + 4 - j, 4) * 128, 128), 128)
        pltpu.make_async_copy(ho.at[rows], ho.at[rows], ex_r.at[j]).wait()

    def other(i, _):
        for u in range(U):
            c = i * U + u
            build_taps(ho, c * 32, 32, go.at[c])
        return 0

    lax.fori_loop(0, CH // U, other, 0)
    stage(1)
    near(go)
    pack_a(1)
    pack_b(1)
    give(lambda s: ys.at[1, s], yt.at[(1 - h) * NB + r], 2)

    def turn_back(role, y):
        y = lax.dot_general(
            flips[role], y, (((1,), (1,)), ((), ())), preferred_element_type=F32
        ).astype(BF16)
        return jnp.dot(y, flips[role], preferred_element_type=F32)

    def source(role, i):
        return jnp.where(h == 1 - role, D // 128 - 1 - i, i)

    own_rows = yt.at[pl.ds(0, NB), 0]
    both_rows = yt.at[pl.ds(0, NB)]
    pltpu.make_async_copy(own_rows, own_rows, y_r.at[0]).wait()
    pltpu.make_async_copy(both_rows, both_rows, y_r.at[2]).wait()
    for i in range(8):
        y = yt[pl.ds(8 * source(0, i), 8), 0, :, :].reshape(128, POS)
        col = pl.ds(128 * i, 128)
        o[0, :, col] = o[0, :, col] * turn_back(0, y)
    pltpu.make_async_copy(own_rows, own_rows, y_r.at[1]).wait()
    pltpu.make_async_copy(weight, wv, in_sem.at[3]).wait()
    pltpu.make_async_copy(pt, pt, y_r.at[3]).wait()
    mine = pl.ds((1 - h) * NB, NB)
    yt[mine, 1, :, :] = (yt[mine, 1, :, :].astype(F32) + pt[...].astype(F32)).astype(BF16)
    for i in range(8):
        y = yt[pl.ds(8 * source(1, i), 8), 1, :, :].reshape(128, POS)
        col = pl.ds(128 * i, 128)
        comb[:, col] = (o[0, :, col] + o[1, :, col] * turn_back(1, y)).astype(BF16)
    for i in range(4):
        col = pl.ds(256 * i, 256)
        out[:, col] = jnp.dot(comb[...], wv[:, col], preferred_element_type=F32).astype(BF16)

    for k in range(2):
        left = z.at[pl.ds(0, NB - 1)]
        pltpu.make_async_copy(left, left, z_s.at[k]).wait()
        left = yt.at[pl.ds(0, NB - 1), 0]
        pltpu.make_async_copy(left, left, y_s.at[k]).wait()
    left = z.at[pl.ds(0, NB), 0]
    pltpu.make_async_copy(left, left, z_s.at[2]).wait()
    left = yt.at[pl.ds(0, NB - 1)]
    pltpu.make_async_copy(left, left, y_s.at[2]).wait()
    pltpu.make_async_copy(ps, ps, y_s.at[3]).wait()
    cross.wait_send()
    for j in range(1, 4):
        mate_copy(j).wait_send()
    pltpu.make_async_copy(hsend.at[0], hsend.at[0], halo_s.at[0]).wait()

    @pl.when(slot > 0)
    def _():
        pltpu.make_async_copy(hsend.at[1], hsend.at[1], halo_s.at[1]).wait()


def per_device(fwd_proj, rev_proj, tokens, short_taps, long_kernel, skip_gain, out_weight):
    vmem = pltpu.VMEM
    dma = pltpu.SemaphoreType.DMA
    anywhere = pl.BlockSpec(memory_space=pl.ANY)
    local = pl.BlockSpec(memory_space=vmem)
    scratch = [
        vmem((2, POS, 3 * D), BF16),
        vmem((2, POS + 8, 3 * D), F32),
        vmem((2, 16, 3 * D), BF16),
        vmem((2, 16, 3 * D), BF16),
        vmem((D // CH, 2, CH, POS), BF16),
        vmem((CH * 64, 128), F32),
        vmem((CH * 64, 128), BF16),
        vmem((CH * 32, 128), BF16),
        vmem((CH * 32, 128), BF16),
        vmem((CH, 1024, 256), BF16),
        vmem((CH, 512, 256), BF16),
        vmem((2, NB, 2, CH, POS), BF16),
        vmem((NB, CH, POS), BF16),
        vmem((NB * CH, POS), F32),
        vmem((NB * CH, POS), F32),
        vmem((NB * CH, POS), F32),
        vmem((NB * CH, POS), F32),
        vmem((NB * CH, POS), F32),
        vmem((2, NB, 2, CH, POS), BF16),
        vmem((NB, CH, POS), BF16),
        vmem((D // CH, 2, CH, POS), BF16),
        vmem((NB, CH, POS), BF16),
        vmem((2, POS, D), F32),
        vmem((POS, D), BF16),
        vmem((D, D), BF16),
        vmem((CH, 8192), F32),
    ]
    scratch += [vmem((8 * NB, 512), BF16)] * U
    scratch += [vmem((4 * 48, 1024), BF16)] * U
    scratch += [vmem((2, 4, ROWS, 128), F32)] * U
    scratch += [vmem((2, 4, 8 + NB, 256), F32)] * U
    scratch += [vmem((4, 48, 256), F32)] * U
    scratch += [
        dma((4,)),
        dma((2,)), dma((2,)),
        dma((4,)), dma((4,)),
        dma((3,)), dma((3,)),
        dma((4,)), dma((4,)),
    ]
    return pl.pallas_call(
        kernel,
        out_shape=jax.ShapeDtypeStruct((POS, D), BF16),
        in_specs=[anywhere, anywhere, local, local, anywhere, local, anywhere],
        out_specs=local,
        scratch_shapes=scratch,
        name="hyena",
        compiler_params=pltpu.CompilerParams(
            collective_id=0, has_side_effects=True, vmem_limit_bytes=60 * 2**20
        ),
    )(
        fwd_proj, rev_proj, tokens.reshape(1, POS), short_taps, long_kernel,
        skip_gain.reshape(1, CH), out_weight,
    )


def solution(mesh):
    in_specs = (
        P(("dp", "ctx"), None),
        P(("dp", "ctx"), None),
        P(("dp", "ctx")),
        P(),
        P("ctx", None),
        P("ctx"),
        P(),
    )
    out_specs = P(("dp", "ctx"), None)
    return jax.shard_map(
        per_device, mesh=mesh, in_specs=in_specs, out_specs=out_specs, check_vma=False
    )
```

profile of v0, /device:TPU:193, one launch (start us, length us, event | category | flops | bytes accessed | tf_op | source)
XLA Modules:
  0.0 67.9 jit_solution(4198516430494521260)
XLA Ops:
  0.0 66.2 %hyena.1 = bf16[128,1024]{1,0:T(8,128)(2,1)} custom-call(bf16[128,3072]{1,0:T(8,128)(2,1)} %fwd.1, bf16[128,3072]{1,0:T(8,128)(2,1)} %rev.1, s32[1,128]{1,0:T(1,128)} %bitcast.2, f32[3,3072]{1,0:T(4,128)} %taps.1, f32[16,8192]{1,0:T(8,128)} %lk.1, f32[1,16]{1,0:T(1,128)} %bitcast.3, bf16[1024,1024]{1,0:T(8,128)(2,1)} %weight.1), custom_call_target="tpu_custom_call" | custom-call | tf_op jit(solution)/shard_map/hyena/pallas_call | solution.py:536
  66.2 1.7 %copy.9 = bf16[128,1024]{1,0:T(8,128)(2,1)} copy(bf16[128,1024]{1,0:T(8,128)(2,1)} %hyena.1) | data formatting | bytes 524288
where the time goes:
time: 68.1 us; the launch traced here: 67.9 us
  Pallas kernels  66.2 us (97%)
  local copies, waits for them, and re-layouts  1.67 us (2%)
    pallas_call x1, Pallas kernels, per_device(): pl.pallas_call(kernel, out_shape=jax.ShapeDtypeStruct((POS, D), BF16), in...  66.2 us
    unnamed x1, local copies, waits for them, and re-layouts  1.67 us

commit v1 on v0

--- a/solution.py
+++ b/solution.py
@@ -15,6 +15,7 @@
 ROWS = PAD + NB + PAD
 LINE = 8
 U = 4
+TILES = 3 * D // 128
 
 
 def eye(flip):
@@ -54,16 +55,16 @@
 
 
 def pieces(turned, start, rows):
-    for w in range(2):
-        for rho in range(4):
-
-            def load(i):
-                return turned[(i - rho) % 4, pl.ds(PAD + start - 8 * w - 2 * i, rows), :]
-
-            v = load(3)
-            for i in (2, 1, 0):
-                v = jnp.where(lane_below(rows, 32 * (i + 1)), load(i), v)
-            yield w, rho, v.astype(BF16)
+    for rho in range(4):
+
+        def load(i):
+            return turned[(i - rho) % 4, pl.ds(PAD + start - 8 - 2 * i, rows + 8), :]
+
+        v = load(3)
+        for i in (2, 1, 0):
+            v = jnp.where(lane_below(rows + 8, 32 * (i + 1)), load(i), v)
+        for w in range(2):
+            yield w, rho, v[8 - 8 * w : 8 - 8 * w + rows].astype(BF16)
 
 
 def overlap(part, at):
@@ -129,7 +130,7 @@
 
 def kernel(
     fwd, rev, tok, taps, lk, skip, weight, out,
-    xin, xf, hsend, halo, z, hf, hk, hn, ho, g, go, rab, rr, sa, sb, sr, ya, yb, ys, ps, yt, pt,
+    xin, xf, hs32, hsend, halo, hr32, z, hf, hk, hn, ho, g, go, rab, rr, sa, sb, sr, ya, yb, keep, ys, ps, yt, pt,
     o, comb, wv, lkv,
     ln0, ln1, ln2, ln3, lf0, lf1, lf2, lf3, tn0, tn1, tn2, tn3, pn0, pn1, pn2, pn3,
     pf0, pf1, pf2, pf3,
@@ -182,17 +183,47 @@
         greet(mate(j))
     lax.fori_loop(1, NB, greet_near, 0)
 
-    for ref in lns + lfs + tns + pns:
-        ref[...] = jnp.zeros_like(ref)
-
     flips = (eye(h == 1), eye(h == 0))
-    for role in range(2):
+
+    def causal(role):
         pltpu.make_async_copy(fwd, xin.at[role], in_sem.at[role]).wait()
         for i in range(6):
             col = pl.ds(512 * i, 512)
             x = jnp.dot(flips[role], xin[role, :, col], preferred_element_type=F32)
             xf[role, 8 : 8 + POS, col] = x
-            hsend[role, :, col] = x[POS - 16 :].astype(BF16)
+        for t in range(TILES):
+            hs32[role, 2 * t : 2 * t + 2, :] = xf[role, 6 + POS : 8 + POS, 128 * t : 128 * t + 128]
+        hsend[role, :, :] = hs32[role, :, :].astype(BF16)
+
+    causal(0)
+
+    pl.semaphore_wait(barrier, 2 * NB - 1 + 4)
+
+    at_end = slot == NB - 1
+    inner = jnp.where(h == 0, r + 1, r - 1)
+    turn = jnp.where(h == 0, 0, NB - 1)
+    next_a = jnp.where(at_end, (1 - h) * NB + turn, h * NB + inner)
+    next_b = h * NB + jnp.where(h == 0, r - 1, r + 1)
+
+    def halo_copy(src, dst, to):
+        return pltpu.make_async_remote_copy(
+            src_ref=hsend.at[src], dst_ref=halo.at[dst], send_sem=halo_s.at[src],
+            recv_sem=halo_r.at[dst], device_id=(dp, to), device_id_type=MESH,
+        )
+
+    @pl.when(at_end)
+    def _():
+        halo_copy(0, 1, next_a).start()
+
+    @pl.when(jnp.logical_not(at_end))
+    def _():
+        halo_copy(0, 0, next_a).start()
+
+    causal(1)
+
+    @pl.when(slot > 0)
+    def _():
+        halo_copy(1, 1, next_b).start()
 
     pltpu.make_async_copy(lk, lkv, in_sem.at[2]).wait()
     diag = lax.broadcasted_iota(I32, (CH, CH), 0) == lax.broadcasted_iota(I32, (CH, CH), 1)
@@ -208,32 +239,6 @@
         hk[64 * c : 64 * c + 64, :] = v
         hn[32 * c : 32 * c + 32, :] = v[:32]
 
-    pl.semaphore_wait(barrier, 2 * NB - 1 + 4)
-
-    at_end = slot == NB - 1
-    inner = jnp.where(h == 0, r + 1, r - 1)
-    turn = jnp.where(h == 0, 0, NB - 1)
-    next_a = jnp.where(at_end, (1 - h) * NB + turn, h * NB + inner)
-    next_b = h * NB + jnp.where(h == 0, r - 1, r + 1)
-
-    def halo_copy(src, dst, to):
-        return pltpu.make_async_remote_copy(
-            src_ref=hsend.at[src], dst_ref=halo.at[dst], send_sem=halo_s.at[src],
-            recv_sem=halo_r.at[dst], device_id=(dp, to), device_id_type=MESH,
-        )
-
-    @pl.when(at_end)
-    def _():
-        halo_copy(0, 1, next_a).start()
-
-    @pl.when(jnp.logical_not(at_end))
-    def _():
-        halo_copy(0, 0, next_a).start()
-
-    @pl.when(slot > 0)
-    def _():
-        halo_copy(1, 1, next_b).start()
-
     share = pl.ds(pl.multiple_of(seat * 128, 128), 128)
     cross = pltpu.make_async_remote_copy(
         src_ref=hn.at[share], dst_ref=ho.at[share], send_sem=ex_s.at[0], recv_sem=ex_r.at[0],
@@ -241,14 +246,6 @@
     )
     cross.start()
 
-    def own(i, _):
-        for u in range(U):
-            c = i * U + u
-            build_taps(hk, c * 64, 64, g.at[c])
-        return 0
-
-    lax.fori_loop(0, CH // U, own, 0)
-
     known = (tok[...] != 4).astype(F32).astype(BF16)
     known = jnp.broadcast_to(known, (16, POS))
 
@@ -263,18 +260,25 @@
         mask = jnp.dot(known, flips[role], preferred_element_type=F32)[0:1]
 
         def tile(i, _):
-            v = short(role, pl.ds(pl.multiple_of(128 * i, 128), 128))
-            q = short(role, pl.ds(pl.multiple_of(128 * i + D, 128), 128))
-            turned = (jnp.transpose(q * v) * mask).astype(BF16)
-            z[pl.ds(8 * i, 8), role, :, :] = turned.reshape(8, CH, POS)
+            for u in range(U):
+                at = U * i + u
+                v = short(role, pl.ds(pl.multiple_of(128 * at, 128), 128))
+                q = short(role, pl.ds(pl.multiple_of(128 * at + D, 128), 128))
+                turned = (jnp.transpose(q * v) * mask).astype(BF16)
+                z[pl.ds(8 * at, 8), role, :, :] = turned.reshape(8, CH, POS)
             return 0
 
-        lax.fori_loop(0, D // 128, tile, 0)
+        lax.fori_loop(0, D // 128 // U, tile, 0)
+
+    def before(role):
+        pltpu.make_async_copy(halo.at[role], halo.at[role], halo_r.at[role]).wait()
+        hr32[role, :, :] = halo[role, :, :].astype(F32)
+        for t in range(TILES):
+            xf[role, 6:8, 128 * t : 128 * t + 128] = hr32[role, 2 * t : 2 * t + 2, :]
 
     @pl.when(slot > 0)
     def _():
-        pltpu.make_async_copy(halo.at[0], halo.at[0], halo_r.at[0]).wait()
-        xf[0, 0:8, :] = halo[0, :, :].astype(F32)[8:16]
+        before(0)
 
     @pl.when(slot == 0)
     def _():
@@ -291,27 +295,22 @@
         ).start()
         return 0
 
-    lax.fori_loop(0, NB, send_far, 0)
-
-    pltpu.make_async_copy(halo.at[1], halo.at[1], halo_r.at[1]).wait()
-    xf[1, 0:8, :] = halo[1, :, :].astype(F32)[8:16]
-    gate(1)
-
-    for k in range(2):
-        group = h if k == 0 else 1 - h
-        pltpu.make_async_copy(z.at[group * NB + r], rab.at[k, slot], z_r.at[k]).start()
-
-        def send_near(j, _, k=k, group=group):
+
+    def send_near(src, dst, sem):
+        pltpu.make_async_copy(src(r), dst, z_r.at[sem]).start()
+
+        def go(j, _):
             who = lax.rem(r + j, NB)
             pltpu.make_async_remote_copy(
-                src_ref=z.at[group * NB + who], dst_ref=rab.at[k, slot],
-                send_sem=z_s.at[k], recv_sem=z_r.at[k],
+                src_ref=src(who), dst_ref=dst, send_sem=z_s.at[sem], recv_sem=z_r.at[sem],
                 device_id=(dp, h * NB + who), device_id_type=MESH,
             ).start()
             return 0
 
-        lax.fori_loop(1, NB, send_near, 0)
-
+        lax.fori_loop(1, NB, go, 0)
+
+    send_near(lambda who: z.at[h * NB + who, 0], rab.at[0, slot, 0], 0)
+    lax.fori_loop(0, NB, send_far, 0)
     cross.wait_recv()
 
     def mate_copy(j):
@@ -323,10 +322,26 @@
     for j in range(1, 4):
         mate_copy(j).start()
 
+    before(1)
+    gate(1)
+    send_near(lambda who: z.at[h * NB + who, 1], rab.at[0, slot, 1], 3)
+    send_near(lambda who: z.at[(1 - h) * NB + who], rab.at[1, slot], 1)
+
+    for ref in lns + lfs + tns + pns:
+        ref[...] = jnp.zeros_like(ref)
+
+    def own(i, _):
+        for u in range(U):
+            c = i * U + u
+            build_taps(hk, c * 64, 64, g.at[c])
+        return 0
+
+    lax.fori_loop(0, CH // U, own, 0)
+
     for role in range(2):
         turned = h == 1 - role
 
-        def gate_out(i, _, role=role, turned=turned):
+        for i in range(D // 128):
             src = jnp.where(turned, D // 128 - 1 - i, i) * 128
             a = short(role, pl.ds(pl.multiple_of(src + 2 * D, 128), 128))
             high = a.astype(BF16)
@@ -335,17 +350,15 @@
             both = jnp.dot(flips[role], both, preferred_element_type=F32).astype(BF16)
             both = jnp.concatenate([both[:, :128], both[:, 128:]], axis=0)
             both = jnp.dot(both, flips[role], preferred_element_type=F32)
-            o[role, :, pl.ds(pl.multiple_of(128 * i, 128), 128)] = both[:POS] + both[POS:]
-            return 0
-
-        lax.fori_loop(0, D // 128, gate_out, 0)
-
-    def stage(k):
-        pltpu.make_async_copy(rab.at[k], rab.at[k], z_r.at[k]).wait()
+            o[role, :, 128 * i : 128 * i + 128] = both[:POS] + both[POS:]
+
+    def stage_a(k):
         for b in range(NB):
-            rows = pl.ds(CH * b, CH)
-            sa[rows, :] = rab[k, b, 0, :, :].astype(F32)
-            sb[rows, :] = rab[k, NB - 1 - b, 1, :, :].astype(F32)
+            sa[CH * b : CH * b + CH, :] = rab[k, b, 0, :, :].astype(F32)
+
+    def stage_b(k):
+        for b in range(NB):
+            sb[CH * b : CH * b + CH, :] = rab[k, NB - 1 - b, 1, :, :].astype(F32)
 
     def near(taps_ref):
         def go(i, _):
@@ -377,9 +390,9 @@
         for b in range(NB):
             ys[k, b, 0, :, :] = ya[CH * b : CH * b + CH, :].astype(BF16)
 
-    def pack_b(k):
+    def pack_b(k, src):
         for b in range(NB):
-            ys[k, NB - 1 - b, 1, :, :] = yb[CH * b : CH * b + CH, :].astype(BF16)
+            ys[k, NB - 1 - b, 1, :, :] = src[CH * b : CH * b + CH, :].astype(BF16)
 
     def give(src, dst, sem):
         pltpu.make_async_copy(src(slot), dst, y_r.at[sem]).start()
@@ -395,7 +408,9 @@
 
         lax.fori_loop(1, NB, go, 0)
 
-    stage(0)
+    half_of = rab.at[0, pl.ds(0, NB), 0]
+    pltpu.make_async_copy(half_of, half_of, z_r.at[0]).wait()
+    stage_a(0)
     far(sa, yb, False)
     for b in range(NB):
         ps[b, :, :] = yb[CH * b : CH * b + CH, :].astype(BF16)
@@ -411,15 +426,12 @@
 
     lax.fori_loop(0, NB, send_part, 0)
 
+    pltpu.make_async_copy(half_of, half_of, z_r.at[3]).wait()
+    stage_b(0)
     near(g)
     pack_a(0)
-    give(lambda s: ys.at[0, s, 0], yt.at[h * NB + r, 0], 0)
-    pltpu.make_async_copy(rr, rr, z_r.at[2]).wait()
-    for b in range(NB):
-        sr[CH * b : CH * b + CH, :] = rr[b, :, :].astype(F32)
-    far(sr, yb, True)
-    pack_b(0)
-    give(lambda s: ys.at[0, s, 1], yt.at[h * NB + r, 1], 1)
+    give(lambda at: ys.at[0, at, 0], yt.at[h * NB + r, 0], 0)
+    keep[...] = yb[...]
 
     for j in range(1, 4):
         rows = pl.ds(pl.multiple_of(lax.rem(seat + 4 - j, 4) * 128, 128), 128)
@@ -432,11 +444,20 @@
         return 0
 
     lax.fori_loop(0, CH // U, other, 0)
-    stage(1)
+    pltpu.make_async_copy(rab.at[1], rab.at[1], z_r.at[1]).wait()
+    stage_a(1)
+    stage_b(1)
     near(go)
     pack_a(1)
-    pack_b(1)
-    give(lambda s: ys.at[1, s], yt.at[(1 - h) * NB + r], 2)
+    pack_b(1, yb)
+    give(lambda at: ys.at[1, at], yt.at[(1 - h) * NB + r], 2)
+
+    pltpu.make_async_copy(rr, rr, z_r.at[2]).wait()
+    for b in range(NB):
+        sr[CH * b : CH * b + CH, :] = rr[b, :, :].astype(F32)
+    far(sr, keep, True)
+    pack_b(0, keep)
+    give(lambda at: ys.at[0, at, 1], yt.at[h * NB + r, 1], 1)
 
     def turn_back(role, y):
         y = lax.dot_general(
@@ -455,24 +476,40 @@
         y = yt[pl.ds(8 * source(0, i), 8), 0, :, :].reshape(128, POS)
         col = pl.ds(128 * i, 128)
         o[0, :, col] = o[0, :, col] * turn_back(0, y)
+    def add_strand(i):
+        y = yt[pl.ds(8 * source(1, i), 8), 1, :, :].reshape(128, POS)
+        col = pl.ds(128 * i, 128)
+        comb[:, col] = (o[0, :, col] + o[1, :, col] * turn_back(1, y)).astype(BF16)
+
+    def project(rows, col):
+        return jnp.dot(comb[:, rows], wv[rows, col], preferred_element_type=F32)
+
+    pltpu.make_async_copy(weight, wv, in_sem.at[3]).wait()
     pltpu.make_async_copy(own_rows, own_rows, y_r.at[1]).wait()
-    pltpu.make_async_copy(weight, wv, in_sem.at[3]).wait()
+    for i in range(4, 8):
+        add_strand(i)
+    for i in range(4):
+        col = pl.ds(256 * i, 256)
+        o[0, :, col] = project(pl.ds(D // 2, D // 2), col) if i >= 2 else o[0, :, col]
     pltpu.make_async_copy(pt, pt, y_r.at[3]).wait()
     mine = pl.ds((1 - h) * NB, NB)
     yt[mine, 1, :, :] = (yt[mine, 1, :, :].astype(F32) + pt[...].astype(F32)).astype(BF16)
-    for i in range(8):
-        y = yt[pl.ds(8 * source(1, i), 8), 1, :, :].reshape(128, POS)
-        col = pl.ds(128 * i, 128)
-        comb[:, col] = (o[0, :, col] + o[1, :, col] * turn_back(1, y)).astype(BF16)
+    for i in range(4):
+        add_strand(i)
     for i in range(4):
         col = pl.ds(256 * i, 256)
-        out[:, col] = jnp.dot(comb[...], wv[:, col], preferred_element_type=F32).astype(BF16)
+        if i >= 2:
+            total = o[0, :, col] + project(pl.ds(0, D // 2), col)
+        else:
+            total = project(pl.ds(0, D), col)
+        out[:, col] = total.astype(BF16)
 
     for k in range(2):
-        left = z.at[pl.ds(0, NB - 1)]
-        pltpu.make_async_copy(left, left, z_s.at[k]).wait()
         left = yt.at[pl.ds(0, NB - 1), 0]
+        pltpu.make_async_copy(left, left, z_s.at[3 * k]).wait()
         pltpu.make_async_copy(left, left, y_s.at[k]).wait()
+    left = z.at[pl.ds(0, NB - 1)]
+    pltpu.make_async_copy(left, left, z_s.at[1]).wait()
     left = z.at[pl.ds(0, NB), 0]
     pltpu.make_async_copy(left, left, z_s.at[2]).wait()
     left = yt.at[pl.ds(0, NB - 1)]
@@ -496,8 +533,10 @@
     scratch = [
         vmem((2, POS, 3 * D), BF16),
         vmem((2, POS + 8, 3 * D), F32),
-        vmem((2, 16, 3 * D), BF16),
-        vmem((2, 16, 3 * D), BF16),
+        vmem((2, 2 * TILES, 128), F32),
+        vmem((2, 2 * TILES, 128), BF16),
+        vmem((2, 2 * TILES, 128), BF16),
+        vmem((2, 2 * TILES, 128), F32),
         vmem((D // CH, 2, CH, POS), BF16),
         vmem((CH * 64, 128), F32),
         vmem((CH * 64, 128), BF16),
@@ -507,6 +546,7 @@
         vmem((CH, 512, 256), BF16),
         vmem((2, NB, 2, CH, POS), BF16),
         vmem((NB, CH, POS), BF16),
+        vmem((NB * CH, POS), F32),
         vmem((NB * CH, POS), F32),
         vmem((NB * CH, POS), F32),
         vmem((NB * CH, POS), F32),
@@ -530,7 +570,7 @@
         dma((4,)),
         dma((2,)), dma((2,)),
         dma((4,)), dma((4,)),
-        dma((3,)), dma((3,)),
+        dma((4,)), dma((4,)),
         dma((4,)), dma((4,)),
     ]
     return pl.pallas_call(

time: 68.1 us -> 62.2 us (0.913)
  the two profiles are of different devices: /device:TPU:193 before, /device:TPU:97 now
where the time goes in v1:
time: 62.2 us; the launch traced here: 62 us
  Pallas kernels  60.3 us (97%)
  local copies, waits for them, and re-layouts  1.67 us (3%)
    pallas_call x1, Pallas kernels, per_device(): pl.pallas_call(kernel, out_shape=jax.ShapeDtypeStruct((POS, D), BF16), in...  60.3 us
    unnamed x1, local copies, waits for them, and re-layouts  1.67 us

profile of v1, /device:TPU:97, one launch (start us, length us, event | category | flops | bytes accessed | tf_op | source)
XLA Modules:
  0.0 62.0 jit_solution(11118883251643509815)
XLA Ops:
  0.0 60.3 %hyena.1 = bf16[128,1024]{1,0:T(8,128)(2,1)} custom-call(bf16[128,3072]{1,0:T(8,128)(2,1)} %fwd.1, bf16[128,3072]{1,0:T(8,128)(2,1)} %rev.1, s32[1,128]{1,0:T(1,128)} %bitcast.2, f32[3,3072]{1,0:T(4,128)} %taps.1, f32[16,8192]{1,0:T(8,128)} %lk.1, f32[1,16]{1,0:T(1,128)} %bitcast.3, bf16[1024,1024]{1,0:T(8,128)(2,1)} %weight.1), custom_call_target="tpu_custom_call" | custom-call | tf_op jit(solution)/shard_map/hyena/pallas_call | solution.py:576
  60.3 1.7 %copy.9 = bf16[128,1024]{1,0:T(8,128)(2,1)} copy(bf16[128,1024]{1,0:T(8,128)(2,1)} %hyena.1) | data formatting | bytes 524288

commit v2 on v1

--- a/solution.py
+++ b/solution.py
@@ -15,6 +15,7 @@
 ROWS = PAD + NB + PAD
 LINE = 8
 U = 4
+W = 16
 TILES = 3 * D // 128
 
 
@@ -132,12 +133,10 @@
     fwd, rev, tok, taps, lk, skip, weight, out,
     xin, xf, hs32, hsend, halo, hr32, z, hf, hk, hn, ho, g, go, rab, rr, sa, sb, sr, ya, yb, keep, ys, ps, yt, pt,
     o, comb, wv, lkv,
-    ln0, ln1, ln2, ln3, lf0, lf1, lf2, lf3, tn0, tn1, tn2, tn3, pn0, pn1, pn2, pn3,
-    pf0, pf1, pf2, pf3,
-    in_sem, halo_s, halo_r, ex_s, ex_r, z_s, z_r, y_s, y_r,
+    *rest,
 ):
-    lns, lfs = (ln0, ln1, ln2, ln3), (lf0, lf1, lf2, lf3)
-    tns, pns, pfs = (tn0, tn1, tn2, tn3), (pn0, pn1, pn2, pn3), (pf0, pf1, pf2, pf3)
+    lns, lfs, tns, pns, pfs = (rest[W * i : W * i + W] for i in range(5))
+    in_sem, halo_s, halo_r, ex_s, ex_r, z_s, z_r, y_s, y_r = rest[5 * W :]
     dp = lax.axis_index("dp")
     ctx = lax.axis_index("ctx")
     h = ctx // NB
@@ -362,29 +361,29 @@
 
     def near(taps_ref):
         def go(i, _):
-            c = i * U
-            for u in range(U):
+            c = i * W
+            for u in range(W):
                 near_rows(c + u, sa, sb, lns[u], tns[u])
-            for u in range(U):
+            for u in range(W):
                 near_dot(taps_ref.at[c + u], lns[u], pns[u])
-            for u in range(U):
+            for u in range(W):
                 near_sum(c + u, pns[u], ya, yb)
             return 0
 
-        lax.fori_loop(0, CH // U, go, 0)
+        go(0, 0)
 
     def far(sig, dst, add):
         def go(i, _):
-            c = i * U
-            for u in range(U):
+            c = i * W
+            for u in range(W):
                 far_rows(c + u, sig, lfs[u], tns[u].at[0])
-            for u in range(U):
+            for u in range(W):
                 far_dot(g.at[c + u], lfs[u], pfs[u])
-            for u in range(U):
+            for u in range(W):
                 far_sum(c + u, pfs[u], dst, add)
             return 0
 
-        lax.fori_loop(0, CH // U, go, 0)
+        go(0, 0)
 
     def pack_a(k):
         for b in range(NB):
@@ -561,11 +560,11 @@
         vmem((D, D), BF16),
         vmem((CH, 8192), F32),
     ]
-    scratch += [vmem((8 * NB, 512), BF16)] * U
-    scratch += [vmem((4 * 48, 1024), BF16)] * U
-    scratch += [vmem((2, 4, ROWS, 128), F32)] * U
-    scratch += [vmem((2, 4, 8 + NB, 256), F32)] * U
-    scratch += [vmem((4, 48, 256), F32)] * U
+    scratch += [vmem((8 * NB, 512), BF16)] * W
+    scratch += [vmem((4 * 48, 1024), BF16)] * W
+    scratch += [vmem((2, 4, ROWS, 128), F32)] * W
+    scratch += [vmem((2, 4, 8 + NB, 256), F32)] * W
+    scratch += [vmem((4, 48, 256), F32)] * W
     scratch += [
         dma((4,)),
         dma((2,)), dma((2,)),

time: 62.2 us -> 60.6 us (0.974)
  Pallas kernels: 60.3 us -> 58.7 us
    pallas_call x1, Pallas kernels: 60.3 us -> 58.7 us  [per_device(): pl.pallas_call(kernel, out_shape=jax.ShapeDtypeStruct((POS, D), BF16), in...]
where the time goes in v2:
time: 60.6 us; the launch traced here: 60.4 us
  Pallas kernels  58.7 us (97%)
  local copies, waits for them, and re-layouts  1.67 us (3%)
    pallas_call x1, Pallas kernels, per_device(): pl.pallas_call(kernel, out_shape=jax.ShapeDtypeStruct((POS, D), BF16), in...  58.7 us
    unnamed x1, local copies, waits for them, and re-layouts  1.67 us

profile of v2, /device:TPU:97, one launch (start us, length us, event | category | flops | bytes accessed | tf_op | source)
XLA Modules:
  0.0 60.4 jit_solution(9492230475765366967)
XLA Ops:
  0.0 58.7 %hyena.1 = bf16[128,1024]{1,0:T(8,128)(2,1)} custom-call(bf16[128,3072]{1,0:T(8,128)(2,1)} %fwd.1, bf16[128,3072]{1,0:T(8,128)(2,1)} %rev.1, s32[1,128]{1,0:T(1,128)} %bitcast.2, f32[3,3072]{1,0:T(4,128)} %taps.1, f32[16,8192]{1,0:T(8,128)} %lk.1, f32[1,16]{1,0:T(1,128)} %bitcast.3, bf16[1024,1024]{1,0:T(8,128)(2,1)} %weight.1), custom_call_target="tpu_custom_call" | custom-call | tf_op jit(solution)/shard_map/hyena/pallas_call | solution.py:575
  58.7 1.7 %copy.9 = bf16[128,1024]{1,0:T(8,128)(2,1)} copy(bf16[128,1024]{1,0:T(8,128)(2,1)} %hyena.1) | data formatting | bytes 524288
